TPU v7x, 32 devices: a whole 2x2x4 slice. The times are simulated.
32 devices in a mesh: beam: 4 (over y, x), chan: 8 (over z, core).
Axes of the slice: x: 2, y: 2, z: 4, core: 2. Of those that a mesh axis runs over, the one named last changes fastest.
Arguments:
- intensities: bfloat16 [32, 8192, 128], P(None, ('beam', 'chan')), may hold values from -6 to 6
- lower_index: int32 [10, 1024], replicated, may hold values from 0 to 511, as said below
- upper_index: int32 [10, 1024], replicated, may hold values from 0 to 511, as said below
- delay_shift: int32 [10, 1024], replicated, may hold values from 0 to 512, as said below
- widths: int32 [8], replicated, may hold values from 1 to 64, as said below
- max_delay: int32 [32], P(('beam', 'chan')), may hold values from 256 to 1023
Outputs:
- snr: float32 [32, 8, 1024], P(('beam', 'chan'))
Inputs may be any that keep to these rules, and one draw needn't show every extreme that they name: `lower_index`: at level l and row r, with d = r mod 2^(l+1), the entry is either floor(d / 2) or min(floor((d + 1) / 2), 2^l - 1). `upper_index`: at level l and row r, with d = r mod 2^(l+1), the entry is either floor(d / 2) or min(floor((d + 1) / 2), 2^l - 1). `delay_shift`: at level l the shift is at most 2^l. Distinct widths; 1 and 64 are always among them.
All inputs are finite; a program needn't handle non-finite values.
Results may differ from a plain program's by a relative error of at most 0.0003.
Values sent between devices are 32-bit elements; how exact they have to be, the bound alone decides.
A program may use at most 64 MiB of HBM per device.

v0:
```python
import functools

import jax
import jax.numpy as jnp
from jax import lax
from jax.experimental import pallas as pl
from jax.experimental.pallas import tpu as pltpu
from jax.sharding import PartitionSpec as P

SUB0 = 8
ROWS = 8
BATCH = 16
CHUNKS = 4
MESH = pl.DeviceIdType.MESH


def take(values, index, axis):
    return jnp.take_along_axis(values, index, axis=axis, mode="promise_in_bounds")


def build_indices(levels, bands, samples, lower_ref, upper_ref, shift_ref, low_at, up_at, time_at):
    depth = 16
    zeros = jnp.zeros((depth - levels, bands), jnp.int32)
    lower = jnp.concatenate([lower_ref[...], zeros], axis=0)
    upper = jnp.concatenate([upper_ref[...], zeros], axis=0)
    shift = jnp.concatenate([shift_ref[...], zeros], axis=0)
    level = lax.broadcasted_iota(jnp.int32, (depth, bands), 0)
    row = lax.broadcasted_iota(jnp.int32, (depth, bands), 1)
    width = jnp.left_shift(jnp.int32(2), level)
    trial = row & (width - 1)
    inside = (row & (ROWS - 1)) - trial
    skip = jnp.where(level >= 4, 4 * (trial // ROWS), 0)
    lower = jnp.where(level <= 2, inside + lower, lower - skip) & (ROWS - 1)
    upper = jnp.where(level <= 2, inside + width // 2 + upper, upper - skip) & (ROWS - 1)
    packed = jnp.concatenate(
        [(lower + ROWS * upper).astype(jnp.float32), jnp.minimum(shift, samples).astype(jnp.float32)],
        axis=0,
    ).astype(jnp.bfloat16)
    entry = lax.broadcasted_iota(jnp.int32, (2 * depth, samples), 0)
    time = lax.broadcasted_iota(jnp.int32, (bands, samples), 1)
    for step in range(levels):
        spread = jnp.where(entry == step, 256.0, jnp.where(entry == depth + step, 1.0, 0.0))
        value = lax.dot_general(
            packed,
            spread.astype(jnp.bfloat16),
            (((0,), (0,)), ((), ())),
            preferred_element_type=jnp.float32,
        ).astype(jnp.int32)
        low_at[step] = (value >> 8) & (ROWS - 1)
        up_at[step] = value >> 11
        time_at[step] = time - (value & 255)


def merge_rows(step, places, source, out, low_at, up_at, time_at):
    samples = out.shape[-1]
    for at in range(0, len(places), BATCH):
        batch = places[at : at + BATCH]
        outs = [pl.ds(row, ROWS) for row, _, _ in batch]
        lowers = [source[pl.ds(row, ROWS)] for _, row, _ in batch]
        uppers = [source[pl.ds(row, ROWS)] for _, _, row in batch]
        whens = [time_at[step, rows] for rows in outs]
        uppers = [take(v, up_at[step, rows], 0) for v, rows in zip(uppers, outs)]
        lowers = [take(v, low_at[step, rows], 0) for v, rows in zip(lowers, outs)]
        uppers = [take(v, when & (samples - 1), 1) for v, when in zip(uppers, whens)]
        for rows, lower, upper, when in zip(outs, lowers, uppers, whens):
            out[rows] = lower + jnp.where(when >= 0, upper, 0.0)


def places_of(step, start, size):
    width = 2 << step
    places = []
    for offset in range(0, size, ROWS):
        row = start + offset
        if width <= ROWS:
            places.append((row, row, row))
            continue
        trial = offset % width
        skip = 4 * (trial // ROWS) if step >= 4 else 0
        base = offset - trial
        places.append((row, start + base + skip, start + base + width // 2 + skip))
    return places


def scores(trials_ref, widths_ref, limit_ref, out_ref, bands, samples, chunk):
    boxes = out_ref.shape[1]
    source = lax.broadcasted_iota(jnp.int32, (samples, 2 * samples), 1) % samples
    target = lax.broadcasted_iota(jnp.int32, (samples, 2 * samples), 0)
    limit = limit_ref[0]
    kernels = []
    for box in range(boxes):
        width = widths_ref[box]
        back = target - source
        hit = jnp.where((back >= 0) & (back < width), 1.0, 0.0)
        mean = jnp.minimum(width, samples - source).astype(jnp.float32) * (1.0 / samples)
        kernels.append((hit - mean).astype(jnp.bfloat16))
    for part in range(bands // chunk):
        trials = trials_ref[pl.ds(part * chunk, chunk)]
        high = trials.astype(jnp.bfloat16)
        low = (trials - high.astype(jnp.float32)).astype(jnp.bfloat16)
        both = jnp.concatenate([high, low], axis=1)
        keep = lax.broadcasted_iota(jnp.int32, (1, chunk), 1) + part * chunk <= limit
        for box in range(boxes):
            offset = lax.dot_general(
                kernels[box], both, (((1,), (1,)), ((), ())), preferred_element_type=jnp.float32
            )
            top = jnp.max(offset, axis=0, keepdims=True)
            spread = jnp.sum(offset * offset, axis=0, keepdims=True) * (1.0 / samples)
            value = jnp.where(keep, top / jnp.sqrt(spread + 1e-05), 0.0)
            out_ref[0, pl.ds(box, 1), pl.ds(part * chunk, chunk)] = value


def kernel(
    beam_count, chan_count, levels,
    x_hbm, lower_hbm, upper_hbm, shift_hbm, widths_hbm, limit_hbm, out_ref,
    x_ref, lower_ref, upper_ref, shift_ref, widths_ref, limit_ref, sums, got, *rest,
):
    states, (low_at, up_at, time_at, load_sem, send_sem, recv_sem) = rest[:levels], rest[levels:]
    count = beam_count * chan_count
    beam, chan = lax.axis_index("beam"), lax.axis_index("chan")
    me = beam * chan_count + chan
    channels, samples = x_ref.shape[1], x_ref.shape[2]
    rows_each = channels // SUB0
    bands = count * rows_each
    beams_each = count // CHUNKS

    def flips(value, size):
        return [(1 << bit) * (1 - 2 * (value // (1 << bit) % 2)) for bit in range(size.bit_length() - 1)]

    beam_flips, chan_flips = flips(beam, beam_count), flips(chan, chan_count)

    def xor(value, steps, mask):
        for bit, step in enumerate(steps):
            if mask >> bit & 1:
                value = value + step
        return value

    turns = [(c, b) for c in range(chan_count) for b in range(beam_count) if (c, b) != (0, 0)]

    def partner(c, b):
        return xor(beam, beam_flips, b), xor(chan, chan_flips, c)

    barrier = pltpu.get_barrier_semaphore()
    loads = [
        pltpu.make_async_copy(
            x_hbm.at[pl.ds(part * beams_each, beams_each)],
            x_ref.at[pl.ds(part * beams_each, beams_each)],
            load_sem.at[part],
        )
        for part in range(CHUNKS)
    ]
    others = [(lower_hbm, lower_ref), (upper_hbm, upper_ref), (shift_hbm, shift_ref), (widths_hbm, widths_ref), (limit_hbm, limit_ref)]
    tables = [
        pltpu.make_async_copy(source, target, load_sem.at[CHUNKS + at])
        for at, (source, target) in enumerate(others)
    ]
    for load in loads + tables:
        load.start()
    for c, b in reversed(turns):
        pl.semaphore_signal(barrier, inc=1, device_id=partner(c, b), device_id_type=MESH)

    band = lax.broadcasted_iota(jnp.int32, (rows_each, channels), 0)
    channel = lax.broadcasted_iota(jnp.int32, (rows_each, channels), 1)
    adder = jnp.where(channel // SUB0 == band, 1.0, 0.0).astype(jnp.bfloat16)
    for part, load in enumerate(loads):
        load.wait()
        for owner in range(part * beams_each, (part + 1) * beams_each):
            sums[owner] = jnp.dot(adder, x_ref[owner], preferred_element_type=jnp.float32)
    for load in tables:
        load.wait()
    pl.semaphore_wait(barrier, count - 1)

    copies = {}
    for c, b in turns:
        beam_to, chan_to = partner(c, b)
        copies[c, b] = pltpu.make_async_remote_copy(
            src_ref=sums.at[beam_to * chan_count + chan_to],
            dst_ref=got.at[me],
            send_sem=send_sem.at[c * beam_count + b],
            recv_sem=recv_sem.at[c * beam_count + b],
            device_id=(beam_to, chan_to),
            device_id_type=MESH,
        )
        copies[c, b].start()
    got[me] = sums[me]
    build_indices(levels, bands, samples, lower_ref, upper_ref, shift_ref, low_at, up_at, time_at)
    for state in states:
        state[pl.ds(bands, ROWS)] = jnp.zeros((ROWS, samples), jnp.float32)

    def level(step, starts, size):
        places = []
        for start in starts:
            places += places_of(step, start, size)
        merge_rows(step, places, states[step - 1], states[step], low_at, up_at, time_at)

    local = rows_each.bit_length() - 1
    group = chan_count * rows_each
    for c in range(chan_count):
        for b in range(beam_count):
            if (c, b) != (0, 0):
                copies[c, b].wait_recv()
        chan_from = xor(chan, chan_flips, c)
        where = pl.multiple_of(chan_from * rows_each, rows_each)
        places = []
        values = []
        for b in range(beam_count):
            for piece in range(0, rows_each, ROWS):
                places.append(b * group + where + piece)
                values.append(got[b * chan_count + chan_from, pl.ds(piece, ROWS)])
        for step in range(min(3, local)):
            rows = [pl.ds(place, ROWS) for place in places]
            whens = [time_at[step, at] for at in rows]
            uppers = [take(v, up_at[step, at], 0) for v, at in zip(values, rows)]
            uppers = [take(v, when & (samples - 1), 1) for v, when in zip(uppers, whens)]
            lowers = [take(v, low_at[step, at], 0) for v, at in zip(values, rows)]
            values = [v + jnp.where(when >= 0, u, 0.0) for v, u, when in zip(lowers, uppers, whens)]
        for place, value in zip(places, values):
            states[2][pl.ds(place, ROWS)] = value
        for step in range(3, local):
            level(step, [b * group + where for b in range(beam_count)], rows_each)
        depth = 0
        while (c + 1) % (2 << depth) == 0 and (2 << depth) <= chan_count:
            size = rows_each * (2 << depth)
            first = chan_from // (2 << depth) * size
            first = pl.multiple_of(first, size)
            level(local + depth, [b * group + first for b in range(beam_count)], size)
            depth += 1
    for step in range(local + chan_count.bit_length() - 1, levels):
        level(step, [0], bands)
    scores(states[levels - 1], widths_ref, limit_ref, out_ref, bands, samples, 256)
    for c, b in turns:
        copies[c, b].wait_send()


def shards(intensities, lower_index, upper_index, delay_shift, widths, max_delay):
    beam_count = lax.axis_size("beam")
    chan_count = lax.axis_size("chan")
    count = beam_count * chan_count
    beams, channels, samples = intensities.shape
    rows_each = channels // SUB0
    bands = count * rows_each
    levels = lower_index.shape[0]
    anywhere = pl.BlockSpec(memory_space=pl.ANY)
    return pl.pallas_call(
        functools.partial(kernel, beam_count, chan_count, levels),
        out_shape=jax.ShapeDtypeStruct((1, widths.shape[0], bands), jnp.float32),
        in_specs=[anywhere] * 6,
        out_specs=pl.BlockSpec(memory_space=pltpu.VMEM),
        scratch_shapes=[
            pltpu.VMEM((beams, channels, samples), intensities.dtype),
            pltpu.VMEM(lower_index.shape, jnp.int32),
            pltpu.VMEM(upper_index.shape, jnp.int32),
            pltpu.VMEM(delay_shift.shape, jnp.int32),
            pltpu.SMEM(widths.shape, jnp.int32),
            pltpu.SMEM(max_delay.shape, jnp.int32),
            pltpu.VMEM((count, rows_each, samples), jnp.float32),
            pltpu.VMEM((count, rows_each, samples), jnp.float32),
        ]
        + [pltpu.VMEM((bands + ROWS, samples), jnp.float32)] * levels
        + [pltpu.VMEM((levels, bands, samples), jnp.int32)] * 3
        + [
            pltpu.SemaphoreType.DMA((CHUNKS + 5,)),
            pltpu.SemaphoreType.DMA((count,)),
            pltpu.SemaphoreType.DMA((count,)),
        ],
        compiler_params=pltpu.CompilerParams(
            collective_id=0, has_side_effects=True, vmem_limit_bytes=56 * 1024 * 1024
        ),
        name="search",
    )(intensities, lower_index, upper_index, delay_shift, widths, max_delay)


def solution(mesh):
    in_specs = (P(None, ("beam", "chan"), None), P(), P(), P(), P(), P(("beam", "chan")))
    out_specs = P(("beam", "chan"), None, None)
    return jax.shard_map(shards, mesh=mesh, in_specs=in_specs, out_specs=out_specs, check_vma=False)
```

profile of v0, /device:TPU:1, one launch (start us, length us, event | category | flops | bytes accessed | tf_op | source)
XLA Modules:
  0.0 24.6 jit_solution(8833528473807428063)
XLA Ops:
  0.7 22.5 %search.1 = f32[1,8,1024]{2,1,0:T(8,128)} custom-call(bf16[32,256,128]{2,1,0:T(8,128)(2,1)} %x_hbm.1, s32[10,1024]{1,0:T(8,128)} %lower_hbm.1, s32[10,1024]{1,0:T(8,128)} %upper_hbm.1, s32[10,1024]{1,0:T(8,128)} %shift_hbm.1, s32[8]{0:T(128)} %widths_hbm.1, s32[1]{0:T(128)S(6)} %copy.8.limit_hbm), custom_call_target="tpu_custom_call" | custom-call | tf_op jit(solution)/shard_map/search/pallas_call | solution.py:243
  23.2 1.4 %copy.9 = f32[1,8,1024]{2,1,0:T(8,128)} copy(f32[1,8,1024]{2,1,0:T(8,128)} %search.1) | data formatting | bytes 65536
where the time goes:
time: 24.8 us; the launch traced here: 24.6 us
  Pallas kernels  22.5 us (91%)
  local copies, waits for them, and re-layouts  1.38 us (6%)
  between operations  0.66 us (3%)
    pallas_call x1, Pallas kernels, shards(): pl.pallas_call(functools.partial(kernel, beam_count, chan_count, levels),...  22.5 us
    unnamed x1, local copies, waits for them, and re-layouts  1.38 us

commit v1 on v0

v1 whole, which is shorter than its diff:
```python
import functools

import jax
import jax.numpy as jnp
from jax import lax
from jax.experimental import pallas as pl
from jax.experimental.pallas import tpu as pltpu
from jax.sharding import PartitionSpec as P

SUB0 = 8
ROWS = 8
BATCH = 16
MESH = pl.DeviceIdType.MESH


def take(values, index, axis):
    return jnp.take_along_axis(values, index, axis=axis, mode="promise_in_bounds")


def source_base(trial, width):
    half = width // 2
    return jnp.minimum(4 * (trial // ROWS), jnp.maximum(half - ROWS, 0))


def build_indices(steps, lower, upper, shift, low_at, up_at, time_at, samples):
    levels, bands = lower.shape
    kept = low_at.shape[1]
    depth = 16
    zeros = jnp.zeros((depth - levels, bands), jnp.int32)
    lower = jnp.concatenate([lower, zeros], axis=0)
    upper = jnp.concatenate([upper, zeros], axis=0)
    shift = jnp.concatenate([shift, zeros], axis=0)
    level = lax.broadcasted_iota(jnp.int32, (depth, bands), 0)
    row = lax.broadcasted_iota(jnp.int32, (depth, bands), 1)
    width = jnp.left_shift(jnp.int32(2), level)
    trial = row & (width - 1)
    inside = (row & (ROWS - 1)) - trial
    skip = source_base(trial, width)
    lower = jnp.where(level <= 2, inside + lower, lower - skip) & (ROWS - 1)
    upper = jnp.where(level <= 2, inside + width // 2 + upper, upper - skip) & (ROWS - 1)
    packed = jnp.concatenate(
        [(lower + ROWS * upper).astype(jnp.float32), jnp.minimum(shift, samples).astype(jnp.float32)],
        axis=0,
    ).astype(jnp.bfloat16)
    entry = lax.broadcasted_iota(jnp.int32, (2 * depth, samples), 0)
    time = lax.broadcasted_iota(jnp.int32, (kept, samples), 1)
    for at, step in enumerate(steps):
        spread = jnp.where(entry == step, 256.0, jnp.where(entry == depth + step, 1.0, 0.0))
        value = lax.dot_general(
            packed,
            spread.astype(jnp.bfloat16),
            (((0,), (0,)), ((), ())),
            preferred_element_type=jnp.float32,
        )[:kept].astype(jnp.int32)
        low_at[at] = (value >> 8) & (ROWS - 1)
        up_at[at] = value >> 11
        time_at[at] = time - (value & 255)


def merge(lowers, uppers, lows, ups, whens, samples):
    uppers = [take(v, up, 0) for v, up in zip(uppers, ups)]
    lowers = [take(v, low, 0) for v, low in zip(lowers, lows)]
    uppers = [take(v, when & (samples - 1), 1) for v, when in zip(uppers, whens)]
    return [v + jnp.where(when >= 0, u, 0.0) for v, u, when in zip(lowers, uppers, whens)]


def places_of(step, start, size, first, last):
    width = 2 << step
    places = []
    for base in range(0, size, width):
        for trial in range(first, last, ROWS):
            skip = min(4 * (trial // ROWS), max(width // 2 - ROWS, 0))
            places.append((base + trial, start + base + trial, start + base + skip, start + base + width // 2 + skip))
    return places


def scores(trials_ref, start, size, widths_ref, limit_ref, out_ref, samples):
    boxes = out_ref.shape[1]
    chunk = min(256, size)
    source = lax.broadcasted_iota(jnp.int32, (samples, 2 * samples), 1) % samples
    target = lax.broadcasted_iota(jnp.int32, (samples, 2 * samples), 0)
    limit = limit_ref[0]
    kernels = []
    for box in range(boxes):
        width = widths_ref[box]
        back = target - source
        hit = jnp.where((back >= 0) & (back < width), 1.0, 0.0)
        mean = jnp.minimum(width, samples - source).astype(jnp.float32) * (1.0 / samples)
        kernels.append((hit - mean).astype(jnp.bfloat16))
    for at in range(start, start + size, chunk):
        trials = trials_ref[pl.ds(at, chunk)]
        high = trials.astype(jnp.bfloat16)
        low = (trials - high.astype(jnp.float32)).astype(jnp.bfloat16)
        both = jnp.concatenate([high, low], axis=1)
        keep = lax.broadcasted_iota(jnp.int32, (1, chunk), 1) + at <= limit
        for box in range(boxes):
            offset = lax.dot_general(
                kernels[box], both, (((1,), (1,)), ((), ())), preferred_element_type=jnp.float32
            )
            top = jnp.max(offset, axis=0, keepdims=True)
            spread = jnp.sum(offset * offset, axis=0, keepdims=True) * (1.0 / samples)
            value = jnp.where(keep, top / jnp.sqrt(spread + 1e-05), 0.0)
            out_ref[0, pl.ds(box, 1), pl.ds(at, chunk)] = value


def kernel(
    beam_count, chan_count, levels, pieces,
    x_hbm, lower_hbm, upper_hbm, shift_hbm, widths_hbm, limit_hbm, out_ref,
    x_ref, lower_ref, upper_ref, shift_ref, widths_ref, limit_ref, work, ready, got, *rest,
):
    count = beam_count * chan_count
    channels, samples = x_ref.shape[1], x_ref.shape[2]
    rows_each = channels // SUB0
    bands = count * rows_each
    local = rows_each.bit_length() - 1
    states, rest = rest[: levels - local], rest[levels - local :]
    low_in, up_in, time_in, low_at, up_at, time_at, load_sem, table_sem, send_sem, recv_sem = rest
    beam, chan = lax.axis_index("beam"), lax.axis_index("chan")
    me = beam * chan_count + chan
    piece_rows = rows_each // pieces

    pair, core = chan // 2, chan % 2
    half = chan_count // 4
    side = pair // half
    far = [(1 - side) * half + at for at in range(half)]
    near = [side * half + (pair + 1 + at) % half for at in range(half)]
    beam_steps = [(1 << bit) * (1 - 2 * (beam // (1 << bit) % 2)) for bit in range(beam_count.bit_length() - 1)]

    def other_beam(mask):
        value = beam
        for bit, step in enumerate(beam_steps):
            if mask >> bit & 1:
                value = value + step
        return value

    def group(pair_to):
        return [(other_beam(mask), pair_to * 2 + (core + turn) % 2) for mask in range(beam_count) for turn in range(2)]

    order = [(pair_to, group(pair_to)) for pair_to in far[:1] + near + far[1:]]
    own = half

    barrier = pltpu.get_barrier_semaphore()
    others = [(lower_hbm, lower_ref), (upper_hbm, upper_ref), (shift_hbm, shift_ref), (widths_hbm, widths_ref), (limit_hbm, limit_ref)]
    tables = [pltpu.make_async_copy(source, target, table_sem.at[at]) for at, (source, target) in enumerate(others)]
    for table in tables:
        table.start()
    loads = []
    for at, (pair_to, _) in enumerate(order):
        loads.append([])
        for mask in range(beam_count):
            rows = pl.ds(other_beam(mask) * chan_count + pair_to * 2, 2)
            load = pltpu.make_async_copy(x_hbm.at[rows], x_ref.at[rows], load_sem.at[at, mask])
            load.start()
            loads[-1].append(load)
    for at, (_, devices) in enumerate(order):
        for place, device in enumerate(devices):
            if (at, place) != (own, 0):
                pl.semaphore_signal(barrier, inc=1, device_id=device, device_id_type=MESH)

    band = lax.broadcasted_iota(jnp.int32, (rows_each, channels), 0)
    channel = lax.broadcasted_iota(jnp.int32, (rows_each, channels), 1)
    adder = jnp.where(channel // SUB0 == band, 1.0, 0.0).astype(jnp.bfloat16)
    for table in tables:
        table.wait()
    block = 128
    first = me * rows_each
    lanes = pl.ds(pl.multiple_of(first // block * block, block), block)
    away = (block - first % block) % block
    mine = [pltpu.roll(ref[:, lanes], away, 1) for ref in (lower_ref, upper_ref, shift_ref)]
    build_indices(range(local), *mine, low_in, up_in, time_in, samples)

    def dedisperse(beams):
        sums = [jnp.dot(adder, x_ref[at], preferred_element_type=jnp.float32) for at in beams]
        tiles = [(at, row) for at in beams for row in range(0, rows_each, ROWS)]
        values = [v[row : row + ROWS] for v in sums for row in range(0, rows_each, ROWS)]
        for step in range(local):
            lows = [low_in[step, pl.ds(row, ROWS)] for _, row in tiles]
            ups = [up_in[step, pl.ds(row, ROWS)] for _, row in tiles]
            whens = [time_in[step, pl.ds(row, ROWS)] for _, row in tiles]
            if step < 3:
                lowers = uppers = values
            else:
                places = places_of(step, 0, rows_each, 0, 2 << step)
                lowers = [work[step - 3, at, pl.ds(row, ROWS)] for at in beams for _, _, row, _ in places]
                uppers = [work[step - 3, at, pl.ds(row, ROWS)] for at in beams for _, _, _, row in places]
            values = merge(lowers, uppers, lows, ups, whens, samples)
            if step >= 2:
                for (at, row), value in zip(tiles, values):
                    if step < local - 1:
                        work[step - 2, at, pl.ds(row, ROWS)] = value
                    else:
                        ready[at, pl.ds(row, ROWS)] = value

    per = max(1, BATCH * ROWS // rows_each)
    for at, (_, devices) in enumerate(order):
        for load in loads[at]:
            load.wait()
        beams = [device[0] * chan_count + device[1] for device in devices]
        for place in range(0, len(beams), per):
            dedisperse(beams[place : place + per])
        if at == 0:
            pl.semaphore_wait(barrier, count - 1)
        for piece in reversed(range(pieces)):
            rows = pl.ds(piece * piece_rows, piece_rows)
            for place, device in enumerate(devices):
                if (at, place) != (own, 0):
                    pltpu.make_async_remote_copy(
                        src_ref=ready.at[beams[place], rows],
                        dst_ref=got.at[me, rows],
                        send_sem=send_sem,
                        recv_sem=recv_sem.at[piece],
                        device_id=device,
                        device_id_type=MESH,
                    ).start()
    got[me] = ready[me]
    build_indices(range(local, levels), lower_ref[...], upper_ref[...], shift_ref[...], low_at, up_at, time_at, samples)

    for piece in reversed(range(pieces)):
        arrived = got.at[pl.ds(0, count - 1), pl.ds(0, piece_rows)]
        pltpu.make_async_copy(arrived, arrived, recv_sem.at[piece]).wait()
        for step in range(local, levels):
            part = (2 << step) // pieces
            places = places_of(step, 0, bands, piece * part, (piece + 1) * part)
            out = states[step - local]

            def read(row):
                if step == local:
                    return got[row // rows_each, pl.ds(row % rows_each, ROWS)]
                return states[step - local - 1][pl.ds(row, ROWS)]

            for at in range(0, len(places), BATCH):
                batch = places[at : at + BATCH]
                rows = [pl.ds(row, ROWS) for row, _, _, _ in batch]
                values = merge(
                    [read(row) for _, _, row, _ in batch],
                    [read(row) for _, _, _, row in batch],
                    [low_at[step - local, row] for row in rows],
                    [up_at[step - local, row] for row in rows],
                    [time_at[step - local, row] for row in rows],
                    samples,
                )
                for row, value in zip(rows, values):
                    out[row] = value
        size = bands // pieces
        scores(states[-1], piece * size, size, widths_ref, limit_ref, out_ref, samples)
    sent = ready.at[pl.ds(0, count - 1)]
    pltpu.make_async_copy(sent, sent, send_sem).wait()


def shards(intensities, lower_index, upper_index, delay_shift, widths, max_delay):
    beam_count = lax.axis_size("beam")
    chan_count = lax.axis_size("chan")
    count = beam_count * chan_count
    beams, channels, samples = intensities.shape
    rows_each = channels // SUB0
    bands = count * rows_each
    levels = lower_index.shape[0]
    local = rows_each.bit_length() - 1
    pieces = rows_each // ROWS
    return pl.pallas_call(
        functools.partial(kernel, beam_count, chan_count, levels, pieces),
        out_shape=pltpu.VMEM((1, widths.shape[0], bands), jnp.float32),
        in_specs=[pl.BlockSpec(memory_space=pltpu.HBM)] * 6,
        out_specs=pl.BlockSpec(memory_space=pltpu.VMEM),
        scratch_shapes=[
            pltpu.VMEM((beams, channels, samples), intensities.dtype),
            pltpu.VMEM(lower_index.shape, jnp.int32),
            pltpu.VMEM(upper_index.shape, jnp.int32),
            pltpu.VMEM(delay_shift.shape, jnp.int32),
            pltpu.SMEM(widths.shape, jnp.int32),
            pltpu.SMEM(max_delay.shape, jnp.int32),
            pltpu.VMEM((max(1, local - 3), count, rows_each, samples), jnp.float32),
            pltpu.VMEM((count, rows_each, samples), jnp.float32),
            pltpu.VMEM((count, rows_each, samples), jnp.float32),
        ]
        + [pltpu.VMEM((bands, samples), jnp.float32)] * (levels - local)
        + [pltpu.VMEM((local, rows_each, samples), jnp.int32)] * 3
        + [pltpu.VMEM((levels - local, bands, samples), jnp.int32)] * 3
        + [
            pltpu.SemaphoreType.DMA((chan_count // 2, beam_count)),
            pltpu.SemaphoreType.DMA((5,)),
            pltpu.SemaphoreType.DMA,
            pltpu.SemaphoreType.DMA((pieces,)),
        ],
        compiler_params=pltpu.CompilerParams(
            collective_id=0, has_side_effects=True, vmem_limit_bytes=56 * 1024 * 1024
        ),
        name="search",
    )(intensities, lower_index, upper_index, delay_shift, widths, max_delay)


def solution(mesh):
    in_specs = (P(None, ("beam", "chan"), None), P(), P(), P(), P(), P(("beam", "chan")))
    out_specs = P(("beam", "chan"), None, None)
    return jax.shard_map(shards, mesh=mesh, in_specs=in_specs, out_specs=out_specs, check_vma=False)
```

time: 24.8 us -> 22.9 us (0.923)
  the two profiles are of different devices: /device:TPU:1 before, /device:TPU:9 now
where the time goes in v1:
time: 22.9 us; the launch traced here: 22.8 us
  Pallas kernels  21.5 us (94%)
  between operations  0.66 us (3%)
  local copies, waits for them, and re-layouts  0.62 us (3%)
    pallas_call x1, Pallas kernels, shards(): pl.pallas_call(functools.partial(kernel, beam_count, chan_count, levels,...  21.5 us
    unnamed x1, local copies, waits for them, and re-layouts  0.62 us

profile of v1, /device:TPU:9, one launch (start us, length us, event | category | flops | bytes accessed | tf_op | source)
XLA Modules:
  0.0 22.8 jit_solution(8226824115825830154)
XLA Ops:
  0.7 21.5 %search.1 = f32[1,8,1024]{2,1,0:T(8,128)S(1)} custom-call(bf16[32,256,128]{2,1,0:T(8,128)(2,1)} %x_hbm.1, s32[10,1024]{1,0:T(8,128)} %lower_hbm.1, s32[10,1024]{1,0:T(8,128)} %upper_hbm.1, s32[10,1024]{1,0:T(8,128)} %shift_hbm.1, s32[8]{0:T(128)} %widths_hbm.1, s32[1]{0:T(128)S(6)} %copy.9.limit_hbm), custom_call_target="tpu_custom_call" | custom-call | tf_op jit(solution)/shard_map/search/pallas_call | solution.py:260
  22.1 0.6 %copy.8 = f32[1,8,1024]{2,1,0:T(8,128)} copy(f32[1,8,1024]{2,1,0:T(8,128)S(1)} %search.1) | data formatting | bytes 65536

commit v2 on v1

--- a/solution.py
+++ b/solution.py
@@ -74,39 +74,62 @@
     return places
 
 
-def scores(trials_ref, start, size, widths_ref, limit_ref, out_ref, samples):
-    boxes = out_ref.shape[1]
-    chunk = min(256, size)
-    source = lax.broadcasted_iota(jnp.int32, (samples, 2 * samples), 1) % samples
-    target = lax.broadcasted_iota(jnp.int32, (samples, 2 * samples), 0)
-    limit = limit_ref[0]
-    kernels = []
+def build_boxes(widths_ref, boxes_ref):
+    boxes, samples, _ = boxes_ref.shape
+    source = lax.broadcasted_iota(jnp.int32, (samples, samples), 1)
+    target = lax.broadcasted_iota(jnp.int32, (samples, samples), 0)
+    back = target - source
     for box in range(boxes):
         width = widths_ref[box]
-        back = target - source
         hit = jnp.where((back >= 0) & (back < width), 1.0, 0.0)
         mean = jnp.minimum(width, samples - source).astype(jnp.float32) * (1.0 / samples)
-        kernels.append((hit - mean).astype(jnp.bfloat16))
+        value = (hit - mean).astype(jnp.bfloat16)
+        boxes_ref[box, :, pl.ds(0, samples)] = value
+        boxes_ref[box, :, pl.ds(samples, samples)] = value
+
+
+def scores(trials_ref, start, size, boxes_ref, limit_ref, out_ref):
+    boxes, samples, _ = boxes_ref.shape
+    chunk = min(256, size)
+    limit = limit_ref[0]
     for at in range(start, start + size, chunk):
         trials = trials_ref[pl.ds(at, chunk)]
         high = trials.astype(jnp.bfloat16)
         low = (trials - high.astype(jnp.float32)).astype(jnp.bfloat16)
         both = jnp.concatenate([high, low], axis=1)
-        keep = lax.broadcasted_iota(jnp.int32, (1, chunk), 1) + at <= limit
+        tops, spreads = [], []
         for box in range(boxes):
             offset = lax.dot_general(
-                kernels[box], both, (((1,), (1,)), ((), ())), preferred_element_type=jnp.float32
+                boxes_ref[box], both, (((1,), (1,)), ((), ())), preferred_element_type=jnp.float32
             )
-            top = jnp.max(offset, axis=0, keepdims=True)
-            spread = jnp.sum(offset * offset, axis=0, keepdims=True) * (1.0 / samples)
-            value = jnp.where(keep, top / jnp.sqrt(spread + 1e-05), 0.0)
-            out_ref[0, pl.ds(box, 1), pl.ds(at, chunk)] = value
+            tops.append(jnp.max(offset, axis=0, keepdims=True))
+            spreads.append(jnp.sum(offset * offset, axis=0, keepdims=True))
+        top = jnp.concatenate(tops, axis=0)
+        spread = jnp.concatenate(spreads, axis=0) * (1.0 / samples)
+        keep = lax.broadcasted_iota(jnp.int32, (boxes, chunk), 1) + at <= limit
+        out_ref[0, :, pl.ds(at, chunk)] = jnp.where(keep, top / jnp.sqrt(spread + 1e-05), 0.0)
+
+
+def schedule(groups, near, turns):
+    cut = max(1, len(turns) // 2)
+    later = [at for at in range(1, groups) if at not in near]
+    items = [(0,)] + [(0, piece, 0) for piece in turns] + [(0, piece, 1) for piece in turns[:cut]]
+    for at in later:
+        items += [(at,)] + [(at, piece, 0) for piece in turns] + [(at, turns[0], 1)]
+    for at in near:
+        items += [(at,)] + [(at, piece, 2) for piece in turns[:cut]]
+    for turn in range(1, len(turns)):
+        ahead = turns[turn + cut - 1 : turn + cut]
+        items += [(0, piece, 1) for piece in ahead]
+        items += [(at, turns[turn], 1) for at in later]
+        items += [(at, piece, 2) for at in near for piece in ahead]
+    return items
 
 
 def kernel(
     beam_count, chan_count, levels, pieces,
     x_hbm, lower_hbm, upper_hbm, shift_hbm, widths_hbm, limit_hbm, out_ref,
-    x_ref, lower_ref, upper_ref, shift_ref, widths_ref, limit_ref, work, ready, got, *rest,
+    x_ref, lower_ref, upper_ref, shift_ref, widths_ref, limit_ref, boxes_ref, work, ready, got, *rest,
 ):
     count = beam_count * chan_count
     channels, samples = x_ref.shape[1], x_ref.shape[2]
@@ -133,13 +156,21 @@
                 value = value + step
         return value
 
-    def group(pair_to):
-        return [(other_beam(mask), pair_to * 2 + (core + turn) % 2) for mask in range(beam_count) for turn in range(2)]
-
-    order = [(pair_to, group(pair_to)) for pair_to in far[:1] + near + far[1:]]
+    def group(pair_to, beams):
+        return [(at, pair_to * 2 + (core + turn) % 2) for at in beams for turn in range(2)]
+
+    fixed = [jnp.int32(at) for at in range(beam_count)]
+    turned = [other_beam(mask) for mask in range(beam_count)]
+    order = [(far[0], group(far[0], fixed))]
+    order += [(pair_to, group(pair_to, turned)) for pair_to in near]
+    order += [(pair_to, group(pair_to, fixed)) for pair_to in far[1:]]
     own = half
 
     barrier = pltpu.get_barrier_semaphore()
+    for at, (_, devices) in enumerate(order):
+        for place, device in enumerate(devices):
+            if (at, place) != (own, 0):
+                pl.semaphore_signal(barrier, inc=1, device_id=device, device_id_type=MESH)
     others = [(lower_hbm, lower_ref), (upper_hbm, upper_ref), (shift_hbm, shift_ref), (widths_hbm, widths_ref), (limit_hbm, limit_ref)]
     tables = [pltpu.make_async_copy(source, target, table_sem.at[at]) for at, (source, target) in enumerate(others)]
     for table in tables:
@@ -152,11 +183,6 @@
             load = pltpu.make_async_copy(x_hbm.at[rows], x_ref.at[rows], load_sem.at[at, mask])
             load.start()
             loads[-1].append(load)
-    for at, (_, devices) in enumerate(order):
-        for place, device in enumerate(devices):
-            if (at, place) != (own, 0):
-                pl.semaphore_signal(barrier, inc=1, device_id=device, device_id_type=MESH)
-
     band = lax.broadcasted_iota(jnp.int32, (rows_each, channels), 0)
     channel = lax.broadcasted_iota(jnp.int32, (rows_each, channels), 1)
     adder = jnp.where(channel // SUB0 == band, 1.0, 0.0).astype(jnp.bfloat16)
@@ -191,31 +217,44 @@
                     else:
                         ready[at, pl.ds(row, ROWS)] = value
 
-    per = max(1, BATCH * ROWS // rows_each)
-    for at, (_, devices) in enumerate(order):
+    def send(at, place, piece):
+        device = order[at][1][place]
+        rows = pl.ds(piece * piece_rows, piece_rows)
+        pltpu.make_async_remote_copy(
+            src_ref=ready.at[device[0] * chan_count + device[1], rows],
+            dst_ref=got.at[me, rows],
+            send_sem=send_sem,
+            recv_sem=recv_sem.at[piece],
+            device_id=device,
+            device_id_type=MESH,
+        ).start()
+
+    def compute(at):
         for load in loads[at]:
             load.wait()
-        beams = [device[0] * chan_count + device[1] for device in devices]
+        beams = [device[0] * chan_count + device[1] for device in order[at][1]]
         for place in range(0, len(beams), per):
             dedisperse(beams[place : place + per])
-        if at == 0:
+
+    per = max(1, BATCH * ROWS // rows_each)
+    turns = list(reversed(range(pieces)))
+    greeted = False
+    for item in schedule(len(order), range(1, half + 1), turns):
+        if len(item) == 1:
+            compute(item[0])
+            continue
+        if not greeted:
             pl.semaphore_wait(barrier, count - 1)
-        for piece in reversed(range(pieces)):
-            rows = pl.ds(piece * piece_rows, piece_rows)
-            for place, device in enumerate(devices):
-                if (at, place) != (own, 0):
-                    pltpu.make_async_remote_copy(
-                        src_ref=ready.at[beams[place], rows],
-                        dst_ref=got.at[me, rows],
-                        send_sem=send_sem,
-                        recv_sem=recv_sem.at[piece],
-                        device_id=device,
-                        device_id_type=MESH,
-                    ).start()
+            greeted = True
+        at, piece, part = item
+        for to in (range(2), range(2, 2 * beam_count), range(2 * beam_count))[part]:
+            if (at, to) != (own, 0):
+                send(at, to, piece)
     got[me] = ready[me]
+    build_boxes(widths_ref, boxes_ref)
     build_indices(range(local, levels), lower_ref[...], upper_ref[...], shift_ref[...], low_at, up_at, time_at, samples)
 
-    for piece in reversed(range(pieces)):
+    for piece in turns:
         arrived = got.at[pl.ds(0, count - 1), pl.ds(0, piece_rows)]
         pltpu.make_async_copy(arrived, arrived, recv_sem.at[piece]).wait()
         for step in range(local, levels):
@@ -242,7 +281,7 @@
                 for row, value in zip(rows, values):
                     out[row] = value
         size = bands // pieces
-        scores(states[-1], piece * size, size, widths_ref, limit_ref, out_ref, samples)
+        scores(states[-1], piece * size, size, boxes_ref, limit_ref, out_ref)
     sent = ready.at[pl.ds(0, count - 1)]
     pltpu.make_async_copy(sent, sent, send_sem).wait()
 
@@ -269,6 +308,7 @@
             pltpu.VMEM(delay_shift.shape, jnp.int32),
             pltpu.SMEM(widths.shape, jnp.int32),
             pltpu.SMEM(max_delay.shape, jnp.int32),
+            pltpu.VMEM((widths.shape[0], samples, 2 * samples), jnp.bfloat16),
             pltpu.VMEM((max(1, local - 3), count, rows_each, samples), jnp.float32),
             pltpu.VMEM((count, rows_each, samples), jnp.float32),
             pltpu.VMEM((count, rows_each, samples), jnp.float32),

time: 22.9 us -> 21.4 us (0.934)
  the two profiles are of different devices: /device:TPU:9 before, /device:TPU:13 now
where the time goes in v2:
time: 21.4 us; the launch traced here: 21.2 us
  Pallas kernels  19.9 us (93%)
  between operations  0.66 us (3%)
  local copies, waits for them, and re-layouts  0.62 us (3%)
    pallas_call x1, Pallas kernels, shards(): pl.pallas_call(functools.partial(kernel, beam_count, chan_count, levels,...  19.9 us
    unnamed x1, local copies, waits for them, and re-layouts  0.62 us

profile of v2, /device:TPU:13, one launch (start us, length us, event | category | flops | bytes accessed | tf_op | source)
XLA Modules:
  0.0 21.2 jit_solution(4911064878687827246)
XLA Ops:
  0.7 19.9 %search.1 = f32[1,8,1024]{2,1,0:T(8,128)S(1)} custom-call(bf16[32,256,128]{2,1,0:T(8,128)(2,1)} %x_hbm.1, s32[10,1024]{1,0:T(8,128)} %lower_hbm.1, s32[10,1024]{1,0:T(8,128)} %upper_hbm.1, s32[10,1024]{1,0:T(8,128)} %shift_hbm.1, s32[8]{0:T(128)} %widths_hbm.1, s32[1]{0:T(128)S(6)} %copy.9.limit_hbm), custom_call_target="tpu_custom_call" | custom-call | tf_op jit(solution)/shard_map/search/pallas_call | solution.py:299
  20.6 0.6 %copy.8 = f32[1,8,1024]{2,1,0:T(8,128)} copy(f32[1,8,1024]{2,1,0:T(8,128)S(1)} %search.1) | data formatting | bytes 65536

commit v3 on v2

--- a/solution.py
+++ b/solution.py
@@ -113,15 +113,16 @@
 def schedule(groups, near, turns):
     cut = max(1, len(turns) // 2)
     later = [at for at in range(1, groups) if at not in near]
-    items = [(0,)] + [(0, piece, 0) for piece in turns] + [(0, piece, 1) for piece in turns[:cut]]
+    items = [(0, 0)] + [(0, piece, 0) for piece in turns] + [(0, 1)] + [(0, piece, 1) for piece in turns[:cut]]
     for at in later:
-        items += [(at,)] + [(at, piece, 0) for piece in turns] + [(at, turns[0], 1)]
+        items += [(at, 2), (at, turns[0], 0), (at, turns[0], 1)] + [(at, piece, 0) for piece in turns[1:2]]
     for at in near:
-        items += [(at,)] + [(at, piece, 2) for piece in turns[:cut]]
+        items += [(at, 2)] + [(at, piece, 2) for piece in turns[:cut]]
     for turn in range(1, len(turns)):
         ahead = turns[turn + cut - 1 : turn + cut]
         items += [(0, piece, 1) for piece in ahead]
-        items += [(at, turns[turn], 1) for at in later]
+        for at in later:
+            items += [(at, turns[turn], 1)] + [(at, piece, 0) for piece in turns[turn + 1 : turn + 2]]
         items += [(at, piece, 2) for at in near for piece in ahead]
     return items
 
@@ -167,22 +168,26 @@
     own = half
 
     barrier = pltpu.get_barrier_semaphore()
+    loads = []
+    for at, (pair_to, devices) in enumerate(order):
+        loads.append([])
+        for place in range(0, len(devices), 2):
+            rows = pl.ds(devices[place][0] * chan_count + pair_to * 2, 2)
+            loads[-1].append(pltpu.make_async_copy(x_hbm.at[rows], x_ref.at[rows], load_sem.at[at, place // 2]))
+    others = [(lower_hbm, lower_ref), (upper_hbm, upper_ref), (shift_hbm, shift_ref), (widths_hbm, widths_ref), (limit_hbm, limit_ref)]
+    tables = [pltpu.make_async_copy(source, target, table_sem.at[at]) for at, (source, target) in enumerate(others)]
+    for table in tables:
+        table.start()
+    for load in loads[0]:
+        load.start()
     for at, (_, devices) in enumerate(order):
         for place, device in enumerate(devices):
             if (at, place) != (own, 0):
                 pl.semaphore_signal(barrier, inc=1, device_id=device, device_id_type=MESH)
-    others = [(lower_hbm, lower_ref), (upper_hbm, upper_ref), (shift_hbm, shift_ref), (widths_hbm, widths_ref), (limit_hbm, limit_ref)]
-    tables = [pltpu.make_async_copy(source, target, table_sem.at[at]) for at, (source, target) in enumerate(others)]
-    for table in tables:
-        table.start()
-    loads = []
-    for at, (pair_to, _) in enumerate(order):
-        loads.append([])
-        for mask in range(beam_count):
-            rows = pl.ds(other_beam(mask) * chan_count + pair_to * 2, 2)
-            load = pltpu.make_async_copy(x_hbm.at[rows], x_ref.at[rows], load_sem.at[at, mask])
+    for group_loads in loads[1:]:
+        for load in group_loads:
             load.start()
-            loads[-1].append(load)
+
     band = lax.broadcasted_iota(jnp.int32, (rows_each, channels), 0)
     channel = lax.broadcasted_iota(jnp.int32, (rows_each, channels), 1)
     adder = jnp.where(channel // SUB0 == band, 1.0, 0.0).astype(jnp.bfloat16)
@@ -229,25 +234,26 @@
             device_id_type=MESH,
         ).start()
 
-    def compute(at):
-        for load in loads[at]:
-            load.wait()
+    def compute(at, part):
+        for mask in sorted({place // 2 for place in parts[part]}):
+            loads[at][mask].wait()
         beams = [device[0] * chan_count + device[1] for device in order[at][1]]
-        for place in range(0, len(beams), per):
-            dedisperse(beams[place : place + per])
-
+        for first in range(parts[part].start, parts[part].stop, per):
+            dedisperse(beams[first : min(first + per, parts[part].stop)])
+
+    parts = (range(2), range(2, 2 * beam_count), range(2 * beam_count))
     per = max(1, BATCH * ROWS // rows_each)
     turns = list(reversed(range(pieces)))
     greeted = False
     for item in schedule(len(order), range(1, half + 1), turns):
-        if len(item) == 1:
-            compute(item[0])
+        if len(item) == 2:
+            compute(*item)
             continue
         if not greeted:
             pl.semaphore_wait(barrier, count - 1)
             greeted = True
         at, piece, part = item
-        for to in (range(2), range(2, 2 * beam_count), range(2 * beam_count))[part]:
+        for to in parts[part]:
             if (at, to) != (own, 0):
                 send(at, to, piece)
     got[me] = ready[me]

time: 21.4 us -> 20.7 us (0.967)
  Pallas kernels: 19.9 us -> 19.3 us
    pallas_call x1, Pallas kernels: 19.9 us -> 19.3 us  [shards(): pl.pallas_call(functools.partial(kernel, beam_count, chan_count, levels,...]
where the time goes in v3:
time: 20.7 us; the launch traced here: 20.5 us
  Pallas kernels  19.3 us (93%)
  between operations  0.66 us (3%)
  local copies, waits for them, and re-layouts  0.62 us (3%)
    pallas_call x1, Pallas kernels, shards(): pl.pallas_call(functools.partial(kernel, beam_count, chan_count, levels,...  19.3 us
    unnamed x1, local copies, waits for them, and re-layouts  0.62 us

profile of v3, /device:TPU:13, one launch (start us, length us, event | category | flops | bytes accessed | tf_op | source)
XLA Modules:
  0.0 20.5 jit_solution(16409763389913836698)
XLA Ops:
  0.7 19.3 %search.1 = f32[1,8,1024]{2,1,0:T(8,128)S(1)} custom-call(bf16[32,256,128]{2,1,0:T(8,128)(2,1)} %x_hbm.1, s32[10,1024]{1,0:T(8,128)} %lower_hbm.1, s32[10,1024]{1,0:T(8,128)} %upper_hbm.1, s32[10,1024]{1,0:T(8,128)} %shift_hbm.1, s32[8]{0:T(128)} %widths_hbm.1, s32[1]{0:T(128)S(6)} %copy.9.limit_hbm), custom_call_target="tpu_custom_call" | custom-call | tf_op jit(solution)/shard_map/search/pallas_call | solution.py:305
  19.9 0.6 %copy.8 = f32[1,8,1024]{2,1,0:T(8,128)} copy(f32[1,8,1024]{2,1,0:T(8,128)S(1)} %search.1) | data formatting | bytes 65536

commit v4 on v3

--- a/solution.py
+++ b/solution.py
@@ -91,23 +91,35 @@
 def scores(trials_ref, start, size, boxes_ref, limit_ref, out_ref):
     boxes, samples, _ = boxes_ref.shape
     chunk = min(256, size)
-    limit = limit_ref[0]
-    for at in range(start, start + size, chunk):
-        trials = trials_ref[pl.ds(at, chunk)]
-        high = trials.astype(jnp.bfloat16)
-        low = (trials - high.astype(jnp.float32)).astype(jnp.bfloat16)
-        both = jnp.concatenate([high, low], axis=1)
-        tops, spreads = [], []
-        for box in range(boxes):
+    steps = []
+
+    def add(at):
+        both, tops, spreads = [], [], []
+
+        def split():
+            trials = trials_ref[pl.ds(at, chunk)]
+            high = trials.astype(jnp.bfloat16)
+            low = (trials - high.astype(jnp.float32)).astype(jnp.bfloat16)
+            both.append(jnp.concatenate([high, low], axis=1))
+
+        def one(box):
             offset = lax.dot_general(
-                boxes_ref[box], both, (((1,), (1,)), ((), ())), preferred_element_type=jnp.float32
+                boxes_ref[box], both[0], (((1,), (1,)), ((), ())), preferred_element_type=jnp.float32
             )
             tops.append(jnp.max(offset, axis=0, keepdims=True))
             spreads.append(jnp.sum(offset * offset, axis=0, keepdims=True))
-        top = jnp.concatenate(tops, axis=0)
-        spread = jnp.concatenate(spreads, axis=0) * (1.0 / samples)
-        keep = lax.broadcasted_iota(jnp.int32, (boxes, chunk), 1) + at <= limit
-        out_ref[0, :, pl.ds(at, chunk)] = jnp.where(keep, top / jnp.sqrt(spread + 1e-05), 0.0)
+
+        def finish():
+            top = jnp.concatenate(tops, axis=0)
+            spread = jnp.concatenate(spreads, axis=0) * (1.0 / samples)
+            keep = lax.broadcasted_iota(jnp.int32, (boxes, chunk), 1) + at <= limit_ref[0]
+            out_ref[0, :, pl.ds(at, chunk)] = jnp.where(keep, top / jnp.sqrt(spread + 1e-05), 0.0)
+
+        steps.extend([split] + [functools.partial(one, box) for box in range(boxes)] + [finish])
+
+    for at in range(start, start + size, chunk):
+        add(at)
+    return steps
 
 
 def schedule(groups, near, turns):
@@ -157,14 +169,14 @@
                 value = value + step
         return value
 
-    def group(pair_to, beams):
-        return [(at, pair_to * 2 + (core + turn) % 2) for at in beams for turn in range(2)]
+    def group(pair_to, beams, lead):
+        return [(at, pair_to * 2 + (lead + turn) % 2) for at in beams for turn in range(2)]
 
     fixed = [jnp.int32(at) for at in range(beam_count)]
     turned = [other_beam(mask) for mask in range(beam_count)]
-    order = [(far[0], group(far[0], fixed))]
-    order += [(pair_to, group(pair_to, turned)) for pair_to in near]
-    order += [(pair_to, group(pair_to, fixed)) for pair_to in far[1:]]
+    order = [(far[0], group(far[0], fixed, 1))]
+    order += [(pair_to, group(pair_to, turned, core)) for pair_to in near]
+    order += [(pair_to, group(pair_to, fixed, 1)) for pair_to in far[1:]]
     own = half
 
     barrier = pltpu.get_barrier_semaphore()
@@ -201,7 +213,11 @@
     build_indices(range(local), *mine, low_in, up_in, time_in, samples)
 
     def dedisperse(beams):
-        sums = [jnp.dot(adder, x_ref[at], preferred_element_type=jnp.float32) for at in beams]
+        sums = []
+        for at in range(0, len(beams), 2):
+            both = jnp.concatenate([x_ref[beam_at] for beam_at in beams[at : at + 2]], axis=1)
+            both = jnp.dot(adder, both, preferred_element_type=jnp.float32)
+            sums += [both[:, lane : lane + samples] for lane in range(0, both.shape[1], samples)]
         tiles = [(at, row) for at in beams for row in range(0, rows_each, ROWS)]
         values = [v[row : row + ROWS] for v in sums for row in range(0, rows_each, ROWS)]
         for step in range(local):
@@ -260,6 +276,7 @@
     build_boxes(widths_ref, boxes_ref)
     build_indices(range(local, levels), lower_ref[...], upper_ref[...], shift_ref[...], low_at, up_at, time_at, samples)
 
+    pending = []
     for piece in turns:
         arrived = got.at[pl.ds(0, count - 1), pl.ds(0, piece_rows)]
         pltpu.make_async_copy(arrived, arrived, recv_sem.at[piece]).wait()
@@ -273,6 +290,10 @@
                     return got[row // rows_each, pl.ds(row % rows_each, ROWS)]
                 return states[step - local - 1][pl.ds(row, ROWS)]
 
+            share = -(-len(pending) // (levels - step))
+            for run in pending[:share]:
+                run()
+            pending = pending[share:]
             for at in range(0, len(places), BATCH):
                 batch = places[at : at + BATCH]
                 rows = [pl.ds(row, ROWS) for row, _, _, _ in batch]
@@ -287,7 +308,9 @@
                 for row, value in zip(rows, values):
                     out[row] = value
         size = bands // pieces
-        scores(states[-1], piece * size, size, boxes_ref, limit_ref, out_ref)
+        pending = scores(states[-1], piece * size, size, boxes_ref, limit_ref, out_ref)
+    for run in pending:
+        run()
     sent = ready.at[pl.ds(0, count - 1)]
     pltpu.make_async_copy(sent, sent, send_sem).wait()
 

time: 20.7 us -> 20.6 us (level)
  Pallas kernels: 19.3 us -> 19 us
    pallas_call x1, Pallas kernels: 19.3 us -> 19 us  [shards(): pl.pallas_call(functools.partial(kernel, beam_count, chan_count, levels,...]
where the time goes in v4:
time: 20.6 us; the launch traced here: 20.3 us
  Pallas kernels  19 us (92%)
  between operations  0.66 us (3%)
  local copies, waits for them, and re-layouts  0.62 us (3%)
    pallas_call x1, Pallas kernels, shards(): pl.pallas_call(functools.partial(kernel, beam_count, chan_count, levels,...  19 us
    unnamed x1, local copies, waits for them, and re-layouts  0.62 us

profile of v4, /device:TPU:13, one launch (start us, length us, event | category | flops | bytes accessed | tf_op | source)
XLA Modules:
  0.0 20.3 jit_solution(17043301381068019100)
XLA Ops:
  0.7 19.0 %search.1 = f32[1,8,1024]{2,1,0:T(8,128)S(1)} custom-call(bf16[32,256,128]{2,1,0:T(8,128)(2,1)} %x_hbm.1, s32[10,1024]{1,0:T(8,128)} %lower_hbm.1, s32[10,1024]{1,0:T(8,128)} %upper_hbm.1, s32[10,1024]{1,0:T(8,128)} %shift_hbm.1, s32[8]{0:T(128)} %widths_hbm.1, s32[1]{0:T(128)S(6)} %copy.9.limit_hbm), custom_call_target="tpu_custom_call" | custom-call | tf_op jit(solution)/shard_map/search/pallas_call | solution.py:328
  19.7 0.6 %copy.8 = f32[1,8,1024]{2,1,0:T(8,128)} copy(f32[1,8,1024]{2,1,0:T(8,128)S(1)} %search.1) | data formatting | bytes 65536

commit v5 on v4

--- a/solution.py
+++ b/solution.py
@@ -9,7 +9,7 @@
 
 SUB0 = 8
 ROWS = 8
-BATCH = 16
+BATCH = 32
 MESH = pl.DeviceIdType.MESH
 
 

time: 20.6 us -> 20.6 us (level)
  no operation moved by 1% of the time
where the time goes in v5:
time: 20.6 us; the launch traced here: 20.3 us
  Pallas kernels  19 us (92%)
  between operations  0.66 us (3%)
  local copies, waits for them, and re-layouts  0.62 us (3%)
    pallas_call x1, Pallas kernels, shards(): pl.pallas_call(functools.partial(kernel, beam_count, chan_count, levels,...  19 us
    unnamed x1, local copies, waits for them, and re-layouts  0.62 us

profile of v5, /device:TPU:13, one launch (start us, length us, event | category | flops | bytes accessed | tf_op | source)
XLA Modules:
  0.0 20.3 jit_solution(5700194126538467235)
XLA Ops:
  0.7 19.0 %search.1 = f32[1,8,1024]{2,1,0:T(8,128)S(1)} custom-call(bf16[32,256,128]{2,1,0:T(8,128)(2,1)} %x_hbm.1, s32[10,1024]{1,0:T(8,128)} %lower_hbm.1, s32[10,1024]{1,0:T(8,128)} %upper_hbm.1, s32[10,1024]{1,0:T(8,128)} %shift_hbm.1, s32[8]{0:T(128)} %widths_hbm.1, s32[1]{0:T(128)S(6)} %copy.9.limit_hbm), custom_call_target="tpu_custom_call" | custom-call | tf_op jit(solution)/shard_map/search/pallas_call | solution.py:328
  19.7 0.6 %copy.8 = f32[1,8,1024]{2,1,0:T(8,128)} copy(f32[1,8,1024]{2,1,0:T(8,128)S(1)} %search.1) | data formatting | bytes 65536
